TPU v7x, 128 devices: a whole 4x4x4 slice. The times are simulated.
128 devices in a mesh: ctx: 8 (over z_hi, x), exp: 16 (over y, z_lo, core).
Axes of the slice: x: 4, y: 4, z: 4 (z_hi: 2, z_lo: 2; z = z_hi * 2 + z_lo), core: 2. Of those that a mesh axis runs over, the one named last changes fastest.
Arguments:
- hidden_in: bfloat16 [16, 1024, 768], P('exp', 'ctx'), may hold values from -6 to 6
- out_grad: bfloat16 [16, 1024, 768], P('exp', 'ctx'), may hold values from -6 to 6
- attn_norm: float32 [768], replicated, may hold values from 0.1 to 1.9
- attn_weight: bfloat16 [3072, 768], P(('ctx', 'exp')), may hold values from -0.8660254 to 0.8660254
- bias_table: float32 [32, 12], replicated, may hold values from -4 to 4
- moe_norm: float32 [768], replicated, may hold values from 0.1 to 1.9
- router: float32 [768, 16], replicated, may hold values from -0.109375 to 0.109375
- expert_in: bfloat16 [16, 768, 3072], P('exp'), may hold values from -0.21875 to 0.21875
- expert_out: bfloat16 [16, 3072, 768], P('exp'), may hold values from -3.5 to 3.5
- expert_ids: int32 [16, 1024, 1], P('exp', 'ctx'), may hold values from 0 to 15; in each aligned block of 128 rows (0 to 127, 128 to 255, ..., all dimensions but the last counted through in order) at most 16 rows name the same one
- block_order: int32 [16, 16], P('exp'), may hold values from 0 to 15, each once within a row
Outputs:
- block_out: bfloat16 [16, 1024, 768], P('exp', 'ctx')
- input_grad: float32 [16, 1024, 768], P('exp', 'ctx')
- attn_norm_grad: float32 [768], replicated
- attn_weight_grad: float32 [3072, 768], P(('ctx', 'exp'))
- bias_table_grad: float32 [32, 12], replicated
- moe_norm_grad: float32 [768], replicated
- router_grad: float32 [768, 16], replicated
- expert_in_grad: float32 [16, 768, 3072], P('exp', 'ctx')
- expert_out_grad: float32 [16, 3072, 768], P('exp', 'ctx')
Inputs may be any that keep to these rules, and one draw needn't show every extreme that they name: `expert_ids`: among the 128 stored rows of one sequence on one index of ctx, at most 16 name the same expert, and in every draw some expert is named by exactly 16 rows of some such block. `block_order`: each sequence's row names every stored block's place once.
All inputs are finite; a program needn't handle non-finite values.
Results may differ from a plain program's by a relative error of at most 0.02.
Values may be sent and summed in bfloat16 or wider, within the bound.
No kernel may reach another device: no remote copies, remote signals or barrier semaphores. Data moves between devices by JAX's collectives and lax.ppermute only.
A program may use at most 128 MiB of HBM per device.

v0:
```python
from functools import partial
import math

import jax
import jax.numpy as jnp
from jax import lax
from jax.experimental import pallas as pl
from jax.experimental.pallas import tpu as pltpu
from jax.sharding import PartitionSpec as P

f32 = jnp.float32
bf16 = jnp.bfloat16
eps_norm = 1e-06
highest = lax.Precision.HIGHEST
bucket_edges = [
    edge if edge <= 16 else int(math.ceil(16.0 * 8.0 ** ((edge - 16) / 16.0)))
    for edge in range(1, 32)
]
masked = -1e30
head_size = 64
own_heads = 3
width_own = own_heads * head_size
half_block = 64
block_count = 16
query_blocks = 8
lanes_step = 256
vmem_bytes = 56 * 1024 * 1024

offsets = [(dz, dx) for dz in range(2) for dx in range(4)]


def gather_perm(dz, dx):
    return [(4 * z + x, 4 * (z ^ dz) + (x + dx) % 4) for z in range(2) for x in range(4)]


def scatter_perm(dz, dx):
    return [(4 * z + x, 4 * (z ^ dz) + (x - dx) % 4) for z in range(2) for x in range(4)]


def dot_nt(left, right):
    return lax.dot_general(left, right, (((1,), (1,)), ((), ())), preferred_element_type=f32)


def dot_tn(left, right):
    return lax.dot_general(left, right, (((0,), (0,)), ((), ())), preferred_element_type=f32)


def dot_nn(left, right):
    return jnp.dot(left, right, preferred_element_type=f32)


def block_places(me_ref, order_ref):
    me = me_ref[0]
    z, x = me // 4, me % 4
    places = []
    for dz, dx in offsets:
        source = 4 * ((z + dz) % 2) + (x - dx + 4) % 4
        places += [order_ref[2 * source], order_ref[2 * source + 1]]
    return places


def tile_class(places, query_block, key_block):
    return jnp.clip(places[query_block] - places[key_block], -1, 3) + 1


def tile_distance(step):
    key_row = lax.broadcasted_iota(jnp.int32, (half_block, 128), 0)
    query_row = lax.broadcasted_iota(jnp.int32, (half_block, 128), 1) & (half_block - 1)
    return step * half_block + query_row - key_row


def attend_kernel(me_ref, order_ref, table_ref, shards_ref, *refs):
    pieces, refs = refs[:8], refs[8:]
    out_ref, q_ref, k_ref, v_ref, log_ref, tiles_ref, weight_ref, project_ref, scores_ref = refs
    exp_count = shards_ref.shape[0]
    for which in range(3):
        weight_ref[which] = jnp.concatenate(
            [
                shards_ref[piece, which].astype(f32)[:, part * width_own : (part + 1) * width_own]
                for part in range(2)
                for piece in range(exp_count)
            ],
            axis=0,
        ).astype(bf16)
    first_piece = (me_ref[0] % 2) * (exp_count // 2)
    for part in range(2):
        project_ref[:, part * 2 * width_own : (part + 1) * 2 * width_own] = jnp.concatenate(
            [
                shards_ref[first_piece + piece, 3 + part].astype(f32)
                for piece in range(exp_count // 2)
            ],
            axis=0,
        ).astype(bf16)
    places = block_places(me_ref, order_ref)
    first_head = (me_ref[0] % 4) * own_heads
    for head in range(own_heads):
        tiles_ref[head, 0] = jnp.full((half_block, 128), masked, f32)
        tiles_ref[head, 4] = jnp.full((half_block, 128), table_ref[31, first_head + head], f32)
    for step in range(3):
        distance = tile_distance(step)
        terms = [
            jnp.full((half_block, 128), table_ref[0, first_head + head], f32)
            for head in range(own_heads)
        ]
        for bucket, edge in enumerate(bucket_edges, 1):
            beyond = distance >= edge
            for head in range(own_heads):
                terms[head] = jnp.where(beyond, table_ref[bucket, first_head + head], terms[head])
        for head in range(own_heads):
            tiles_ref[head, step + 1] = (
                jnp.where(distance >= 0, terms[head], masked) if step == 0 else terms[head]
            )
    for index, piece in enumerate(pieces):
        rows = slice(index * piece.shape[0], (index + 1) * piece.shape[0])
        normed = piece[...]
        k_ref[rows] = dot_nn(normed, weight_ref[1]).astype(bf16)
        v_ref[rows] = dot_nn(normed, weight_ref[2]).astype(bf16)
        if index < 4:
            q_ref[rows] = dot_nn(normed, weight_ref[0]).astype(bf16) * bf16(0.125)
    first_half = lax.broadcasted_iota(jnp.int32, (half_block, 128), 1) < half_block
    for head in range(own_heads):
        columns = slice(head * head_size, (head + 1) * head_size)
        keys, values = k_ref[:, columns], v_ref[:, columns]
        for part in range(query_blocks * half_block // lanes_step):
            lanes = slice(part * lanes_step, (part + 1) * lanes_step)
            add_bias(places, tiles_ref, scores_ref, first_half, head, part,
                     dot_nt(keys, q_ref[lanes, columns]))
            scores = scores_ref[...]
            peak = jnp.max(scores, axis=0, keepdims=True)
            raised = jnp.exp(scores - peak)
            total = jnp.sum(raised, axis=0, keepdims=True)
            probs = (raised * (1.0 / total)).astype(bf16)
            out_ref[columns, lanes] = dot_tn(values, probs).astype(bf16)
            log_ref[head, :, lanes] = peak + jnp.log(total)


def add_bias(places, tiles_ref, scores_ref, first_half, head, part, raw):
    for key_block in range(block_count):
        rows = slice(key_block * half_block, (key_block + 1) * half_block)
        for group in range(lanes_step // 128):
            lanes = slice(group * 128, (group + 1) * 128)
            query_block = part * (lanes_step // half_block) + 2 * group
            left = tile_class(places, query_block, key_block)
            right = tile_class(places, query_block + 1, key_block)
            scores_ref[rows, lanes] = raw[rows, lanes] + jnp.where(
                first_half, tiles_ref[head, left], tiles_ref[head, right]
            )


def attend_back_kernel(
    me_ref, order_ref, q_ref, k_ref, v_ref, log_ref, tiles_ref, project_ref, *refs,
):
    grad_pieces, refs = refs[:4], refs[4:]
    dq_ref, dk_ref, dv_ref, query_ref, keep_ref, give_ref, table_ref = refs[:7]
    scores_ref, sums_ref, grad_ref = refs[7:]
    places = block_places(me_ref, order_ref)
    size = query_blocks * half_block // 4
    for index, piece in enumerate(grad_pieces):
        rows = slice(index * size, (index + 1) * size)
        grad_ref[rows] = dot_nt(piece[:size], project_ref[...]).astype(bf16)
    first_half = lax.broadcasted_iota(jnp.int32, (half_block, 128), 1) < half_block
    buckets = []
    for step in range(3):
        distance = tile_distance(step)
        counted = jnp.zeros((half_block, 128), jnp.int32)
        for edge in bucket_edges:
            counted = counted + (distance >= edge).astype(jnp.int32)
        buckets.append(counted)
    for head in range(own_heads):
        columns = slice(head * head_size, (head + 1) * head_size)
        keys, values = k_ref[:, columns], v_ref[:, columns]
        sums_ref[...] = jnp.zeros_like(sums_ref)
        key_sum = value_sum = None
        for part in range(query_blocks * half_block // lanes_step):
            lanes = slice(part * lanes_step, (part + 1) * lanes_step)
            queries, grads = q_ref[lanes, columns], grad_ref[lanes, columns]
            add_bias(places, tiles_ref, scores_ref, first_half, head, part, dot_nt(keys, queries))
            probs = jnp.exp(scores_ref[...] - log_ref[head, :, lanes])
            probs_grad = dot_nt(values, grads)
            row_dot = jnp.sum(probs * probs_grad, axis=0, keepdims=True)
            score_grad = probs * (probs_grad - row_dot)
            scores_ref[...] = score_grad
            low = score_grad.astype(bf16)
            value_part = dot_nn(probs.astype(bf16), grads)
            key_part = dot_nn(low, queries)
            value_sum = value_part if value_sum is None else value_sum + value_part
            key_sum = key_part if key_sum is None else key_sum + key_part
            dq_ref[columns, lanes] = (dot_tn(keys, low) * 0.125).astype(bf16)
            for key_block in range(block_count):
                rows = slice(key_block * half_block, (key_block + 1) * half_block)
                for group in range(lanes_step // 128):
                    query_block = part * (lanes_step // half_block) + 2 * group
                    left = tile_class(places, query_block, key_block)
                    right = tile_class(places, query_block + 1, key_block)
                    tile = scores_ref[rows, group * 128 : (group + 1) * 128]
                    sums_ref[left] += jnp.where(first_half, tile, 0.0)
                    sums_ref[right] += jnp.where(first_half, 0.0, tile)
        dk_ref[:, columns] = key_sum.astype(bf16)
        dv_ref[:, columns] = value_sum.astype(bf16)
        for bucket in range(32):
            found = [jnp.where(buckets[step] == bucket, sums_ref[step + 1], 0.0) for step in range(3)]
            if bucket == 31:
                found.append(sums_ref[4])
            table_ref[head, bucket : bucket + 1, :] = jnp.sum(sum(found), axis=0, keepdims=True)

    dq, dk, dv = dq_ref[...], dk_ref[...], dv_ref[...]
    half = query_blocks * half_block
    query_ref[...] = dq.T
    keys_values = jnp.concatenate([dk.astype(f32), dv.astype(f32)], axis=1).astype(bf16)
    keep_ref[...] = keys_values[:half]
    give_ref[...] = keys_values[half:]


def pieces_kernel(
    me_ref, dq_ref, dk_ref, dv_ref, table_ref, weight_ref, attended_ref, *refs,
):
    pieces, grad_pieces, chunk_ref, normed_ref = refs[:8], refs[8:12], refs[12], refs[13]
    size = pieces[0].shape[0]
    for index, piece in enumerate(pieces):
        normed_ref[index * size : (index + 1) * size] = piece[...]
    project_grad = jnp.zeros((width_own, normed_ref.shape[1]), f32)
    for index, piece in enumerate(grad_pieces):
        rows = slice(index * size, (index + 1) * size)
        project_grad = project_grad + dot_nn(attended_ref[:, rows], piece[:size])
    normed = normed_ref[...]
    half = normed.shape[0] // 2
    exp_count = chunk_ref.shape[0]
    shard_rows = 24
    flipped = [
        dot_nn(dq_ref[...], normed[:half]),
        dot_tn(dk_ref[...], normed),
        dot_tn(dv_ref[...], normed),
    ]
    norm_sum = jnp.zeros((1, normed.shape[1]), f32)
    straight = []
    for which in range(3):
        weight_t = weight_ref[which].astype(f32).T
        norm_sum = norm_sum + jnp.sum(flipped[which] * weight_t, axis=0, keepdims=True)
        straight.append(flipped[which].T)
    wide = 2 * width_own
    row = lax.broadcasted_iota(jnp.int32, (16, wide), 0)
    heads = [jnp.sum(table_ref[head].T, axis=0, keepdims=True) for head in range(own_heads)]
    table_row = jnp.concatenate(
        [
            heads[head] * (me_ref[0] % 4 == group).astype(f32)
            for group in range(4)
            for head in range(own_heads)
        ],
        axis=1,
    )
    small_rows = [table_row, norm_sum[:, :wide], norm_sum[:, wide:]]
    early = sum(piece[size:].astype(f32) for piece in grad_pieces)
    for index in range(5):
        for block in range(2):
            small_rows.append(early[index : index + 1, block * wide : (block + 1) * wide])
    small_slab = jnp.zeros((16, wide), f32)
    for index, small_row in enumerate(small_rows):
        small_slab = jnp.where(row == index, small_row, small_slab)
    odd = me_ref[0] % 2
    for piece in range(exp_count):
        slabs = []
        for which in range(3):
            starts = [(part * exp_count + piece) * shard_rows for part in range(2)]
            slabs.append(
                jnp.concatenate(
                    [straight[which][start : start + shard_rows] for start in starts], axis=1
                )
            )
        start = (piece % 8) * shard_rows
        mine = (odd == piece // 8).astype(f32)
        for block in range(2):
            slabs.append(
                project_grad[start : start + shard_rows, block * wide : (block + 1) * wide] * mine
            )
        chunk_ref[piece] = jnp.concatenate(slabs + [small_slab], axis=0).astype(bf16)


def rows_kernel(query_ref, keep_ref, taken_ref, weight_ref, own_ref, *low_refs):
    size = own_ref.shape[0]
    for index in range(4):
        rows = slice(index * size, (index + 1) * size)
        both = keep_ref[rows].astype(f32) + taken_ref[rows].astype(f32)
        part = dot_nt(query_ref[rows], weight_ref[0])
        part = part + dot_nt(both[:, :width_own].astype(bf16), weight_ref[1])
        part = part + dot_nt(both[:, width_own:].astype(bf16), weight_ref[2])
        if index:
            low_refs[index - 1][...] = part.astype(bf16)
        else:
            own_ref[...] = part


def rows_grad(query, keep, taken, weights):
    size, width = query.shape[0] // 4, weights.shape[1]
    return pl.pallas_call(
        rows_kernel,
        out_shape=[jax.ShapeDtypeStruct((size, width), kind) for kind in (f32, bf16, bf16, bf16)],
        in_specs=[in_vmem()] * 4,
        out_specs=[in_vmem()] * 4,
        compiler_params=pltpu.CompilerParams(vmem_limit_bytes=vmem_bytes),
        name="rows_grad",
    )(query, keep, taken, weights)


def place_kernel(columns_ref, placed_ref):
    tile = columns_ref.shape[2] // 2
    for source in range(4):
        both = columns_ref[source].astype(f32) + columns_ref[4 + source].astype(f32)
        for part in range(2):
            start = (4 * part + source) * tile
            placed_ref[:, start : start + tile] = both[:, part * tile : (part + 1) * tile]


def place(columns):
    count, rows, double = columns.shape
    return pl.pallas_call(
        place_kernel,
        out_shape=jax.ShapeDtypeStruct((rows, count * double // 2), f32),
        in_specs=[in_vmem()],
        out_specs=in_vmem(),
        compiler_params=pltpu.CompilerParams(vmem_limit_bytes=vmem_bytes),
        name="place",
    )(columns)


def gelu_both(u):
    slope = math.sqrt(2.0 / math.pi)
    square = u * u
    bent = jnp.tanh(slope * u * (1.0 + 0.044715 * square))
    halved = 0.5 * (1.0 + bent)
    derivative = halved + 0.5 * u * (1.0 - bent * bent) * (slope * (1.0 + 0.134145 * square))
    return u * halved, derivative


def expert_kernel(rows_ref, in_ref, out_ref, result_ref, sum_ref):
    step = pl.program_id(0)
    width = in_ref.shape[0]
    rows_in, rows_grad = rows_ref[:, :width], rows_ref[:, width:]
    hidden, derivative = gelu_both(dot_nn(rows_in, in_ref[...]))
    produced = dot_nn(hidden.astype(bf16), out_ref[...])
    pre_grad = (dot_nt(rows_grad, out_ref[...]) * derivative).astype(bf16)
    row_grad = dot_nt(pre_grad, in_ref[...])

    @pl.when(step == 0)
    def _():
        sum_ref[:, :width] = produced
        sum_ref[:, width:] = row_grad

    @pl.when(step > 0)
    def _():
        sum_ref[:, :width] += produced
        sum_ref[:, width:] += row_grad

    @pl.when(step == pl.num_programs(0) - 1)
    def _():
        result_ref[...] = sum_ref[...].astype(bf16)


def expert(rows, w_in, w_out):
    count, double = rows.shape
    width, hidden = w_in.shape
    tile = hidden // 3
    return pl.pallas_call(
        expert_kernel,
        grid=(3,),
        out_shape=jax.ShapeDtypeStruct((count, double), bf16),
        in_specs=[
            pl.BlockSpec((count, double), lambda i: (0, 0)),
            pl.BlockSpec((width, tile), lambda i: (0, i)),
            pl.BlockSpec((tile, width), lambda i: (i, 0)),
        ],
        out_specs=pl.BlockSpec((count, double), lambda i: (0, 0)),
        scratch_shapes=[pltpu.VMEM((count, double), f32)],
        compiler_params=pltpu.CompilerParams(vmem_limit_bytes=vmem_bytes),
        name="expert",
    )(rows, w_in, w_out)


def expert_grads_kernel(
    me_ref, rows_a, rows_b, rows_c, rows_d, in_ref, out_ref,
    columns_ref, own_ref, other_ref,
):
    step = pl.program_id(0)
    width = in_ref.shape[0]
    in_sum = out_sum = None
    for piece in (rows_a, rows_b, rows_c, rows_d):
        rows_in, rows_grad = piece[:, :width], piece[:, width:]
        hidden, derivative = gelu_both(dot_nn(rows_in, in_ref[...]))
        pre_grad = (dot_nt(rows_grad, out_ref[...]) * derivative).astype(bf16)
        out_part = dot_tn(hidden.astype(bf16), rows_grad)
        in_part = dot_tn(rows_in, pre_grad)
        out_sum = out_part if out_sum is None else out_sum + out_part
        in_sum = in_part if in_sum is None else in_sum + in_part
    count = columns_ref.shape[0]
    in_rows = width // count
    columns_ref[...] = in_sum.astype(bf16).reshape(count, in_rows, in_sum.shape[1])

    @pl.when(step == me_ref[0] // 4)
    def _():
        own_ref[...] = out_sum

    @pl.when(step != me_ref[0] // 4)
    def _():
        other_ref[...] = out_sum.astype(bf16)


def expert_grads(me, pieces, w_in, w_out):
    count, double = pieces[0].shape
    width, hidden = w_in.shape
    tile = hidden // 8
    in_rows = width // 8
    return pl.pallas_call(
        expert_grads_kernel,
        grid_spec=pltpu.PrefetchScalarGridSpec(
            num_scalar_prefetch=1,
            grid=(2,),
            in_specs=[pl.BlockSpec((count, double), lambda i, me: (0, 0))] * 4
            + [
                pl.BlockSpec((width, tile), lambda i, me: (0, 4 * i + me[0] % 4)),
                pl.BlockSpec((tile, width), lambda i, me: (4 * i + me[0] % 4, 0)),
            ],
            out_specs=[
                pl.BlockSpec((8, in_rows, tile), lambda i, me: (0, 0, i)),
                pl.BlockSpec((tile, width), lambda i, me: (0, 0)),
                pl.BlockSpec((tile, width), lambda i, me: (0, 0)),
            ],
        ),
        out_shape=[
            jax.ShapeDtypeStruct((8, in_rows, 2 * tile), bf16),
            jax.ShapeDtypeStruct((tile, width), f32),
            jax.ShapeDtypeStruct((tile, width), bf16),
        ],
        compiler_params=pltpu.CompilerParams(vmem_limit_bytes=vmem_bytes),
        name="expert_grads",
    )(me, *pieces, w_in, w_out)


def in_smem():
    return pl.BlockSpec(memory_space=pltpu.SMEM)


def in_vmem():
    return pl.BlockSpec(memory_space=pltpu.VMEM)


def attend(me, order, table, shards, pieces):
    rows = 8 * pieces[0].shape[0]
    width = pieces[0].shape[1]
    shapes = [
        ((width_own, rows // 2), bf16),
        ((rows // 2, width_own), bf16),
        ((rows, width_own), bf16),
        ((rows, width_own), bf16),
        ((own_heads, 1, rows // 2), f32),
        ((own_heads, 5, half_block, 128), f32),
        ((3, width, width_own), bf16),
        ((width_own, width), bf16),
    ]
    return pl.pallas_call(
        attend_kernel,
        out_shape=[jax.ShapeDtypeStruct(shape, kind) for shape, kind in shapes],
        in_specs=[in_smem()] * 3 + [in_vmem()] * 9,
        out_specs=[in_vmem()] * len(shapes),
        scratch_shapes=[pltpu.VMEM((rows, lanes_step), f32)],
        compiler_params=pltpu.CompilerParams(vmem_limit_bytes=vmem_bytes),
        name="attend",
    )(me, order, table, shards, *pieces)


def attend_back(me, order, q, k, v, logs, tiles, project, grads):
    rows = k.shape[0]
    half = rows // 2
    shapes = [
        ((width_own, half), bf16),
        ((rows, width_own), bf16),
        ((rows, width_own), bf16),
        ((half, width_own), bf16),
        ((half, 2 * width_own), bf16),
        ((half, 2 * width_own), bf16),
        ((own_heads, 32, 128), f32),
    ]
    return pl.pallas_call(
        attend_back_kernel,
        out_shape=[jax.ShapeDtypeStruct(shape, kind) for shape, kind in shapes],
        in_specs=[in_smem()] * 2 + [in_vmem()] * 10,
        out_specs=[in_vmem()] * len(shapes),
        scratch_shapes=[
            pltpu.VMEM((rows, lanes_step), f32),
            pltpu.VMEM((5, half_block, 128), f32),
            pltpu.VMEM((half, width_own), bf16),
        ],
        compiler_params=pltpu.CompilerParams(vmem_limit_bytes=vmem_bytes),
        name="attend_back",
    )(me, order, q, k, v, logs, tiles, project, *grads)


def weight_pieces(me, dq, dk, dv, table, weights, attended, pieces, grads):
    rows, width = dk.shape[0], weights.shape[1]
    return pl.pallas_call(
        pieces_kernel,
        out_shape=jax.ShapeDtypeStruct((16, 136, 2 * width_own), bf16),
        in_specs=[in_smem()] + [in_vmem()] * 18,
        out_specs=in_vmem(),
        scratch_shapes=[pltpu.VMEM((rows, width), bf16)],
        compiler_params=pltpu.CompilerParams(vmem_limit_bytes=vmem_bytes),
        name="weight_pieces",
    )(me, dq, dk, dv, table, weights, attended, *pieces, *grads)


def regroup_kernel(me_ref, chunk_ref, payload_ref):
    shard_rows, wide = 24, 2 * width_own
    total = chunk_ref[0].astype(f32)
    for source in range(1, chunk_ref.shape[0]):
        total = total + chunk_ref[source].astype(f32)
    small = total[5 * shard_rows :]
    for target in range(8):
        if target < 6:
            start = (target // 2) * shard_rows
            left = (target % 2) * width_own
            part = total[start : start + shard_rows, left : left + width_own]
            part = jnp.concatenate([part, jnp.zeros((shard_rows, width_own), f32)], axis=1)
            parts = [part, jnp.zeros((shard_rows, wide), f32), small]
        else:
            mine = ((me_ref[0] % 4) // 2 == target - 6).astype(f32)
            parts = [total[3 * shard_rows : 5 * shard_rows] * mine, small]
        payload_ref[target] = jnp.concatenate(parts, axis=0).astype(bf16)


def regroup(me, chunks):
    return pl.pallas_call(
        regroup_kernel,
        out_shape=jax.ShapeDtypeStruct((8, 64, 2 * width_own), bf16),
        in_specs=[in_smem(), in_vmem()],
        out_specs=in_vmem(),
        compiler_params=pltpu.CompilerParams(vmem_limit_bytes=vmem_bytes),
        name="regroup",
    )(me, chunks)


def finish_kernel(me_ref, last_ref, gain_ref, weight_ref, table_ref, norm_ref, moe_ref, router_ref):
    shard_rows, wide = 24, 2 * width_own
    parts = [last_ref[source].astype(f32) for source in range(8)]
    as_qkv = jnp.concatenate(
        [
            parts[block][:shard_rows, :width_own] + parts[4 + block][:shard_rows, :width_own]
            for block in range(4)
        ],
        axis=1,
    )
    total = sum(parts[1:], parts[0])
    as_out = jnp.concatenate([total[:shard_rows], total[shard_rows : 2 * shard_rows]], axis=1)
    weight_ref[...] = jnp.where(me_ref[0] < 6, as_qkv, as_out)
    small = total[2 * shard_rows :]
    for head in range(table_ref.shape[0]):
        table_ref[head : head + 1] = small[0:1, head * 32 : (head + 1) * 32]
    for block in range(6):
        line, left = block // 3, (block % 3) * 128
        norm_ref[block : block + 1] = small[1 + line : 2 + line, left : left + 128]
        moe_ref[block : block + 1] = small[11 + line : 12 + line, left : left + 128]
    norm_ref[...] = norm_ref[...] / gain_ref[...]
    for block in range(4):
        early = (parts[block] + parts[4 + block])[2 * shard_rows :]
        for index in range(4):
            line = 3 + 2 * index
            router_ref[4 * block + index : 4 * block + index + 1, :wide] = early[line : line + 1]
            router_ref[4 * block + index : 4 * block + index + 1, wide:] = early[line + 1 : line + 2]


def finish(me, last, gain):
    width = gain.size
    shapes = [(24, width), (12, 32), gain.shape, gain.shape, (16, width)]
    return pl.pallas_call(
        finish_kernel,
        out_shape=[jax.ShapeDtypeStruct(shape, f32) for shape in shapes],
        in_specs=[in_smem(), in_vmem(), in_vmem()],
        out_specs=[in_vmem()] * len(shapes),
        compiler_params=pltpu.CompilerParams(vmem_limit_bytes=vmem_bytes),
        name="finish",
    )(me, last, gain)


def swap(chunks, axis):
    return lax.all_to_all(chunks, axis, split_axis=0, concat_axis=0, tiled=True)


def spread(part, axis, count):
    return swap(jnp.broadcast_to(part[None], (count,) + part.shape), axis)


def gelu(u):
    return jax.nn.gelu(u, approximate=True)


def body(
    hidden_in,
    out_grad,
    attn_norm,
    attn_weight,
    bias_table,
    moe_norm,
    router,
    expert_in,
    expert_out,
    expert_ids,
    block_order,
):
    width = attn_norm.shape[0]
    ctx_count, exp_count = 8, 16
    me = lax.axis_index("ctx")
    x_index = me % 4
    z_index = me // 4
    tokens = hidden_in.shape[1]
    expert_count = router.shape[1]
    capacity = 2 * tokens // expert_count
    me_array = me.astype(jnp.int32).reshape(1)
    order = block_order[0]

    inputs = hidden_in[0].astype(f32)
    scale_one = lax.rsqrt(jnp.mean(inputs * inputs, axis=-1, keepdims=True) + eps_norm)
    scaled_one = inputs * scale_one
    normed_low = (scaled_one * attn_norm).astype(bf16)
    pieces = [normed_low] + [
        lax.ppermute(normed_low, "ctx", gather_perm(dz, dx)) for dz, dx in offsets[1:]
    ]
    shard_rows = attn_weight.shape[0]
    by_ctx = spread(attn_weight, "ctx", ctx_count)
    qkv_own = lax.dynamic_slice_in_dim(by_ctx[:6], x_index * width_own, width_own, 2)
    out_own = lax.dynamic_index_in_dim(by_ctx, 6 + x_index // 2, 0, False)
    wide = 2 * width_own
    part_own = jnp.stack(
        [jnp.concatenate([qkv_own[2 * which], qkv_own[2 * which + 1]], axis=1) for which in range(3)]
        + [out_own[:, :wide], out_own[:, wide:]]
    )
    part_own, *pieces[1:5] = lax.optimization_barrier((part_own, *pieces[1:5]))
    by_exp = spread(part_own, "exp", exp_count)
    attended, q, k, v, logs, tiles, qkv_weights, out_weight = attend(
        me_array, order, bias_table, by_exp, pieces
    )
    out_partial = dot_tn(attended, out_weight)
    out_blocks = out_partial.reshape(4, tokens, width)
    mid = inputs + out_blocks[0]
    out_low = out_blocks.astype(bf16)
    for dx in range(1, 4):
        mid = mid + lax.ppermute(out_low[dx], "ctx", scatter_perm(0, dx)).astype(f32)

    scale_two = lax.rsqrt(jnp.mean(mid * mid, axis=-1, keepdims=True) + eps_norm)
    scaled_two = mid * scale_two
    normed_two = scaled_two * moe_norm
    logits = jnp.dot(normed_two, router, precision=highest)
    router_prob = jax.nn.softmax(logits, axis=-1)
    chosen = expert_ids[0, :, 0]
    picked = chosen[:, None] == jnp.arange(expert_count, dtype=jnp.int32)[None, :]
    gate = jnp.sum(jnp.where(picked, router_prob, 0.0), axis=-1, keepdims=True)
    earlier = (
        jnp.arange(tokens, dtype=jnp.int32)[:, None] > jnp.arange(tokens, dtype=jnp.int32)[None, :]
    )
    same = chosen[:, None] == chosen[None, :]
    slot = jnp.sum((earlier & same).astype(jnp.int32), axis=1)
    targets = chosen * capacity + slot
    placing = (
        targets[:, None] == jnp.arange(expert_count * capacity, dtype=jnp.int32)[None, :]
    ).astype(bf16)
    cotangent = out_grad[0].astype(f32)
    sent = (gate * cotangent).astype(bf16)
    both = jnp.concatenate([normed_two.astype(bf16), sent], axis=1)
    outgoing = dot_tn(placing, both).astype(bf16).reshape(exp_count, capacity, 2 * width)
    arrived = swap(outgoing, "exp").reshape(exp_count * capacity, 2 * width)

    gathered = [arrived] + [
        lax.ppermute(arrived, "ctx", gather_perm(0, dx)) for dx in range(1, 4)
    ]

    w_in, w_out = expert_in[0], expert_out[0]
    returned = swap(expert(arrived, w_in, w_out).reshape(exp_count, capacity, 2 * width), "exp")
    returned, gathered[1], gathered[3] = lax.optimization_barrier(
        (returned, gathered[1], gathered[3])
    )
    home = dot_nn(placing, returned.reshape(exp_count * capacity, 2 * width))
    expert_result, rows_back = home[:, :width], home[:, width:]

    block_out = (mid + gate * expert_result).astype(bf16)[None]
    gate_grad = jnp.sum(cotangent * expert_result, axis=-1, keepdims=True)
    prob_grad = jnp.where(picked, gate_grad, 0.0)
    logit_grad = router_prob * (
        prob_grad - jnp.sum(router_prob * prob_grad, axis=-1, keepdims=True)
    )
    router_local = lax.dot_general(
        logit_grad, normed_two, (((0,), (0,)), ((), ())), precision=highest
    )
    normed_two_grad = rows_back + lax.dot_general(
        logit_grad, router, (((1,), (1,)), ((), ())), precision=highest
    )
    moe_norm_local = jnp.sum(normed_two_grad * scaled_two, axis=0)
    gained = normed_two_grad * moe_norm
    mid_grad = cotangent + scale_two * (
        gained - scaled_two * jnp.mean(gained * scaled_two, axis=-1, keepdims=True)
    )
    attn_grad = mid_grad.astype(bf16)
    quarter = jnp.arange(width, dtype=jnp.int32)[None] // width_own
    attn_grads = []
    for dx in range(4):
        target = (x_index + dx) % 4
        small = jnp.concatenate(
            [
                lax.dynamic_slice_in_dim(router_local, target * 4, 4, 0),
                jnp.where(quarter == target, moe_norm_local[None], 0.0),
                jnp.zeros((11, width), f32),
            ],
            axis=0,
        )
        part = jnp.concatenate([attn_grad, small.astype(bf16)], axis=0)
        attn_grads.append(lax.ppermute(part, "ctx", gather_perm(0, dx)) if dx else part)

    in_columns, out_own_grad, out_other_grad = expert_grads(
        me_array, gathered, w_in, w_out
    )
    in_columns, *attn_grads = lax.optimization_barrier((in_columns, *attn_grads))
    columns_last = swap(in_columns, "ctx")
    dq, dk, dv, query_grad, kept, given, table_local = attend_back(
        me_array, order, q, k, v, logs, tiles, out_weight, attn_grads
    )
    taken = lax.ppermute(given, "ctx", gather_perm(1, 0))
    chunks = weight_pieces(
        me_array, dq, dk, dv, table_local, qkv_weights, attended, pieces, attn_grads
    )
    chunks, taken, columns_last = lax.optimization_barrier((chunks, taken, columns_last))
    payload = regroup(me_array, swap(chunks, "exp"))

    normed_grad, *row_low = rows_grad(query_grad, kept, taken, qkv_weights)
    row_parts = [
        lax.ppermute(low_part, "ctx", scatter_perm(0, index + 1))
        for index, low_part in enumerate(row_low)
    ]
    *row_parts, _ = lax.optimization_barrier((*row_parts, payload[0, :1, :1]))
    for part in row_parts:
        normed_grad = normed_grad + part.astype(f32)
    out_other_grad, _ = lax.optimization_barrier((out_other_grad, payload[0, :1, :1]))
    out_taken = lax.ppermute(out_other_grad, "ctx", gather_perm(1, 0))
    expert_in_grad = place(columns_last)
    expert_out_grad = (out_own_grad + out_taken.astype(f32))[None]
    gained_one = normed_grad * attn_norm
    input_grad = (
        mid_grad
        + scale_one
        * (gained_one - scaled_one * jnp.mean(gained_one * scaled_one, axis=-1, keepdims=True))
    )[None]

    attn_weight_grad, table_row, norm_row, moe_row, router_rows = finish(
        me_array, swap(payload, "ctx"), attn_norm.reshape(-1, 128)
    )
    bias_table_grad = table_row.T
    attn_norm_grad = norm_row.reshape(-1)
    moe_norm_grad = moe_row.reshape(-1)
    router_grad = router_rows.T
    return (
        block_out,
        input_grad,
        attn_norm_grad,
        attn_weight_grad,
        bias_table_grad,
        moe_norm_grad,
        router_grad,
        expert_in_grad[None],
        expert_out_grad,
    )


def solution(mesh):
    placed = (
        P("exp", "ctx", None),
        P("exp", "ctx", None),
        P(),
        P(("ctx", "exp"), None),
        P(),
        P(),
        P(),
        P("exp", None, None),
        P("exp", None, None),
        P("exp", "ctx", None),
        P("exp", None),
    )
    return jax.shard_map(
        body,
        mesh=mesh,
        in_specs=placed,
        out_specs=(
            P("exp", "ctx", None),
            P("exp", "ctx", None),
            P(),
            P(("ctx", "exp"), None),
            P(),
            P(),
            P(),
            P("exp", "ctx", None),
            P("exp", "ctx", None),
        ),
        check_vma=False,
    )
```

profile of v0, /device:TPU:0, one launch (start us, length us, event | category | flops | bytes accessed | tf_op | source)
XLA Modules:
  0.0 248.3 jit_solution(1169627715953937820)
XLA Ops:
  2.2 7.7 %all-to-all-start = ((bf16[8,24,768]{2,1,0:T(8,128)(2,1)}), bf16[8,24,768]{2,1,0:T(8,128)(2,1)S(1)}, u32[]{:S(2)}, u32[]{:S(2)}) async-start(bf16[8,24,768]{2,1,0:T(8,128)(2,1)} %broadcast_in_dim.32), calls=%async_computation | async-start | bytes 589824 | tf_op jit(solution)/shard_map/all_to_all | solution.py:582
  26.7 5.0 %all-to-all-start.1 = ((bf16[16,5,24,384]{3,2,1,0:T(8,128)(2,1)}), bf16[16,5,24,384]{3,2,1,0:T(8,128)(2,1)S(1)}, u32[]{:S(2)}, u32[]{:S(2)}) async-start(bf16[16,5,24,384]{3,2,1,0:T(8,128)(2,1)} %broadcast_in_dim.33), calls=%async_computation.1 | async-start | bytes 2949120 | tf_op jit(solution)/shard_map/all_to_all | solution.py:582
  31.8 4.1 %collective-permute-start.4 = (bf16[128,768]{1,0:T(8,128)(2,1)S(1)}, bf16[128,768]{1,0:T(8,128)(2,1)S(1)}, u32[]{:S(2)}, u32[]{:S(2)}) collective-permute-start(bf16[128,768]{1,0:T(8,128)(2,1)S(1)} %fusion.3.refs_0_), channel_id=1, source_target_pairs={{0,80},{16,96},{32,112},{48,64},{64,16},{80,32},{96,48},{112,0},{1... | collective-permute-start | bytes 589832 | tf_op jit(solution)/shard_map/ppermute | solution.py:622
  37.5 4.7 %collective-permute-start.6 = (bf16[128,768]{1,0:T(8,128)(2,1)S(1)}, bf16[128,768]{1,0:T(8,128)(2,1)S(1)}, u32[]{:S(2)}, u32[]{:S(2)}) collective-permute-start(bf16[128,768]{1,0:T(8,128)(2,1)S(1)} %fusion.3.refs_0_), channel_id=1, source_target_pairs={{0,112},{16,64},{32,80},{48,96},{64,48},{80,0},{96,16},{112,32},{1... | collective-permute-start | bytes 589832 | tf_op jit(solution)/shard_map/ppermute | solution.py:622
  43.1 5.8 %collective-permute-done.4.refs_5_ = bf16[128,768]{1,0:T(8,128)(2,1)S(1)} collective-permute-done((bf16[128,768]{1,0:T(8,128)(2,1)S(1)}, bf16[128,768]{1,0:T(8,128)(2,1)S(1)}, u32[]{:S(2)}, u32[]{:S(2)}) %collective-permute-start.4) | collective-permute-done | bytes 196640 | tf_op jit(solution)/shard_map/ppermute | solution.py:622
  48.9 9.3 %collective-permute-done.5.refs_6_ = bf16[128,768]{1,0:T(8,128)(2,1)S(1)} collective-permute-done((bf16[128,768]{1,0:T(8,128)(2,1)S(1)}, bf16[128,768]{1,0:T(8,128)(2,1)S(1)}, u32[]{:S(2)}, u32[]{:S(2)}) %collective-permute-start.5) | collective-permute-done | bytes 196640 | tf_op jit(solution)/shard_map/ppermute | solution.py:622
  58.1 4.1 %collective-permute-done.6.refs_7_ = bf16[128,768]{1,0:T(8,128)(2,1)S(1)} collective-permute-done((bf16[128,768]{1,0:T(8,128)(2,1)S(1)}, bf16[128,768]{1,0:T(8,128)(2,1)S(1)}, u32[]{:S(2)}, u32[]{:S(2)}) %collective-permute-start.6) | collective-permute-done | bytes 196640 | tf_op jit(solution)/shard_map/ppermute | solution.py:622
  63.4 10.1 %attend.1 = (bf16[192,512]{1,0:T(8,128)(2,1)}, bf16[512,192]{1,0:T(8,128)(2,1)}, bf16[1024,192]{1,0:T(8,128)(2,1)}, bf16[1024,192]{1,0:T(8,128)(2,1)}, f32[3,1,5...) custom-call(s32[1]{0:T(128)} %bitcast.1.me_ref, ...), custom_call_target="tpu_custom_call" | custom-call | tf_op jit(solution)/shard_map/attend/pallas_call | solution.py:458
  79.7 8.6 %collective-permute-done.9 = bf16[128,768]{1,0:T(8,128)(2,1)S(1)} collective-permute-done((bf16[128,768]{1,0:T(8,128)(2,1)S(1)}, bf16[128,768]{1,0:T(8,128)(2,1)S(1)}, u32[]{:S(2)}, u32[]{:S(2)}) %collective-permute-start.9) | collective-permute-done | bytes 196640 | tf_op jit(solution)/shard_map/ppermute | solution.py:643
  90.3 17.6 %all_to_all.35 = bf16[16,16,1536]{2,1,0:T(8,128)(2,1)} all-to-all(bf16[16,16,1536]{2,1,0:T(8,128)(2,1)S(1)} %bitcast.84), channel_id=1, replica_groups=mesh['ctx'=8,'exp'=16] {'exp'}, dimensions={0} | all-to-all | bytes 1572864 | tf_op jit(solution)/shard_map/all_to_all | solution.py:582
  111.1 9.5 %expert.1 = bf16[256,1536]{1,0:T(8,128)(2,1)} custom-call(bf16[256,1536]{1,0:T(8,128)(2,1)} %bitcast.19.rows_ref.rows_a, bf16[768,3072]{1,0:T(8,128)(2,1)} %bitcast.79, bf16[3072,768]{1,0:T(8,128)(2,1)} %bitcast.81), custom_call_target="tpu_custom_call" | custom-call | tf_op jit(solution)/shard_map/expert/pallas_call | solution.py:362
  120.6 3.6 %all-to-all-start.3 = ((bf16[16,16,1536]{2,1,0:T(8,128)(2,1)}), bf16[16,16,1536]{2,1,0:T(8,128)(2,1)S(1)}, u32[]{:S(2)}, u32[]{:S(2)}) async-start(bf16[16,16,1536]{2,1,0:T(8,128)(2,1)} %bitcast.85), calls=%async_computation.3 | async-start | bytes 1572864 | tf_op jit(solution)/shard_map/all_to_all | solution.py:582
  125.6 12.3 %all-to-all-done.3 = bf16[16,16,1536]{2,1,0:T(8,128)(2,1)S(1)} async-done(((bf16[16,16,1536]{2,1,0:T(8,128)(2,1)}), bf16[16,16,1536]{2,1,0:T(8,128)(2,1)S(1)}, u32[]{:S(2)}, u32[]{:S(2)}) %all-to-all-start.3) | async-done | bytes 786464 | tf_op jit(solution)/shard_map/all_to_all | solution.py:582
  147.4 10.8 %expert_grads.1 = (bf16[8,96,768]{2,1,0:T(8,128)(2,1)}, f32[384,768]{1,0:T(8,128)}, bf16[384,768]{1,0:T(8,128)(2,1)}) custom-call(s32[1]{0:T(128)} %bitcast.1.me_ref, bf16[256,1536]{1,0:T(8,128)(2,1)} %bitcast.19.rows_ref.rows_a, bf16[256,1536]{1,0:T(8,128)(2,1)} %copy-done.23, bf16[256,1536]{1,0:T(8,128)(2,1)} %collective-permute-done.12.rows_c, ...), custom_call_target="tpu_custom_call" | custom-call | tf_op jit(solution)/shard_map/expert_grads/pallas_call | solution.py:411
  158.3 6.1 %all-to-all-start.4 = ((bf16[8,96,768]{2,1,0:T(8,128)(2,1)}), bf16[8,96,768]{2,1,0:T(8,128)(2,1)S(1)}, u32[]{:S(2)}, u32[]{:S(2)}) async-start(bf16[8,96,768]{2,1,0:T(8,128)(2,1)} %get-tuple-element.84), calls=%async_computation.4 | async-start | bytes 2359296 | tf_op jit(solution)/shard_map/all_to_all | solution.py:582
  164.4 10.8 %attend_back.1 = (bf16[192,512]{1,0:T(8,128)(2,1)}, bf16[1024,192]{1,0:T(8,128)(2,1)}, bf16[1024,192]{1,0:T(8,128)(2,1)}, bf16[512,192]{1,0:T(8,128)(2,1)}, bf16...) custom-call(s32[1]{0:T(128)} %bitcast.1.me_ref, s32[16]{0:T(128)} %bitcast.94, ...), custom_call_target="tpu_custom_call" | custom-call | tf_op jit(solution)/shard_map/attend_back/pallas_call | solution.py:481
  178.7 5.3 %weight_pieces.1 = bf16[16,136,384]{2,1,0:T(8,128)(2,1)} custom-call(s32[1]{0:T(128)} %bitcast.1.me_ref, bf16[192,512]{1,0:T(8,128)(2,1)} %get-tuple-element.78.dq_ref, bf16[1024,192]{1,0:T(8,128)(2,1)} %get-tuple-element.79.dk_ref, bf16[1024,192]{1,0:T(8,128)(2,1)} %get-tuple-element.80.dv_ref, f32[3,32,128]{2,1,0:T(8,128)} %get-tuple-element.81.table_ref, ...), custom_call_target="tpu_custom_call" | custom-call | tf_op jit(solution)/shard_map/weight_pieces/pallas_call | solution.py:498
  183.9 5.8 %collective-permute-done.16.taken_ref = bf16[512,384]{1,0:T(8,128)(2,1)} collective-permute-done((bf16[512,384]{1,0:T(8,128)(2,1)}, bf16[512,384]{1,0:T(8,128)(2,1)}, u32[]{:S(2)}, u32[]{:S(2)}) %collective-permute-start.16) | collective-permute-done | bytes 393248 | tf_op jit(solution)/shard_map/ppermute | solution.py:721
  190.8 3.9 %all-to-all-start.5 = ((bf16[16,136,384]{2,1,0:T(8,128)(2,1)}), bf16[16,136,384]{2,1,0:T(8,128)(2,1)S(1)}, u32[]{:S(2)}, u32[]{:S(2)}) async-start(bf16[16,136,384]{2,1,0:T(8,128)(2,1)} %weight_pieces.1), calls=%async_computation.5 | async-start | bytes 3342336 | tf_op jit(solution)/shard_map/all_to_all | solution.py:582
  194.6 4.0 %rows_grad.1 = (f32[128,768]{1,0:T(8,128)}, bf16[128,768]{1,0:T(8,128)(2,1)}, bf16[128,768]{1,0:T(8,128)(2,1)}, bf16[128,768]{1,0:T(8,128)(2,1)}) custom-call(bf16[512,192]{1,0:T(8,128)(2,1)} %get-tuple-element.76.query_ref, bf16[512,384]{1,0:T(8,128)(2,1)} %get-tuple-element.77.keep_ref, bf16[512,384]{1,0:T(8,128)(2,1)} %collective-permute-done.16.taken_ref, ...), custom_call_target="tpu_custom_call" | custom-call | tf_op jit(solution)/shard_map/rows_grad/pallas_call | solution.py:294
  203.7 14.0 %all-to-all-done.5.chunk_ref = bf16[16,136,384]{2,1,0:T(8,128)(2,1)S(1)} async-done(((bf16[16,136,384]{2,1,0:T(8,128)(2,1)}), bf16[16,136,384]{2,1,0:T(8,128)(2,1)S(1)}, u32[]{:S(2)}, u32[]{:S(2)}) %all-to-all-start.5) | async-done | bytes 1671200 | tf_op jit(solution)/shard_map/all_to_all | solution.py:582
  221.4 4.1 %all-to-all-start.6 = ((bf16[8,64,384]{2,1,0:T(8,128)(2,1)}), bf16[8,64,384]{2,1,0:T(8,128)(2,1)S(1)}, u32[]{:S(2)}, u32[]{:S(2)}) async-start(bf16[8,64,384]{2,1,0:T(8,128)(2,1)} %regroup.1), calls=%async_computation.6 | async-start | bytes 786432 | tf_op jit(solution)/shard_map/all_to_all | solution.py:582
  225.6 3.6 %collective-permute-start.20 = (bf16[384,768]{1,0:T(8,128)(2,1)}, bf16[384,768]{1,0:T(8,128)(2,1)}, u32[]{:S(2)}, u32[]{:S(2)}) collective-permute-start(bf16[384,768]{1,0:T(8,128)(2,1)} %get-tuple-element.102), channel_id=1, source_target_pairs={{0,64},{16,80},{32,96},{48,112},{64,0},{80,16},{96,32},{112,48},{1... | collective-permute-start | bytes 1769480 | tf_op jit(solution)/shard_map/ppermute | solution.py:737
  238.0 8.2 %collective-permute-done.20 = bf16[384,768]{1,0:T(8,128)(2,1)} collective-permute-done((bf16[384,768]{1,0:T(8,128)(2,1)}, bf16[384,768]{1,0:T(8,128)(2,1)}, u32[]{:S(2)}, u32[]{:S(2)}) %collective-permute-start.20) | collective-permute-done | bytes 589856 | tf_op jit(solution)/shard_map/ppermute | solution.py:737
  (139 shorter events, 68.3 us)
Async XLA Ops:
  2.2 19.0 %all-to-all-start = ((bf16[8,24,768]{2,1,0:T(8,128)(2,1)}), bf16[8,24,768]{2,1,0:T(8,128)(2,1)S(1)}, u32[]{:S(2)}, u32[]{:S(2)}) async-start(bf16[8,24,768]{2,1,0:T(8,128)(2,1)} %broadcast_in_dim.32), calls=%async_computation | async-start | bytes 589824 | tf_op jit(solution)/shard_map/all_to_all | solution.py:582
  14.1 11.2 %collective-permute-start.1 = (bf16[128,768]{1,0:T(8,128)(2,1)S(1)}, bf16[128,768]{1,0:T(8,128)(2,1)S(1)}, u32[]{:S(2)}, u32[]{:S(2)}) collective-permute-start(bf16[128,768]{1,0:T(8,128)(2,1)S(1)} %fusion.3.refs_0_), channel_id=1, source_target_pairs={{0,32},{16,48},{32,0},{48,16},{64,96},{80,112},{96,64},{112,80},{1... | collective-permute-start | bytes 589832 | tf_op jit(solution)/shard_map/ppermute | solution.py:622
  26.7 35.5 %all-to-all-start.1 = ((bf16[16,5,24,384]{3,2,1,0:T(8,128)(2,1)}), bf16[16,5,24,384]{3,2,1,0:T(8,128)(2,1)S(1)}, u32[]{:S(2)}, u32[]{:S(2)}) async-start(bf16[16,5,24,384]{3,2,1,0:T(8,128)(2,1)} %broadcast_in_dim.33), calls=%async_computation.1 | async-start | bytes 2949120 | tf_op jit(solution)/shard_map/all_to_all | solution.py:582
  31.8 17.1 %collective-permute-start.4 = (bf16[128,768]{1,0:T(8,128)(2,1)S(1)}, bf16[128,768]{1,0:T(8,128)(2,1)S(1)}, u32[]{:S(2)}, u32[]{:S(2)}) collective-permute-start(bf16[128,768]{1,0:T(8,128)(2,1)S(1)} %fusion.3.refs_0_), channel_id=1, source_target_pairs={{0,80},{16,96},{32,112},{48,64},{64,16},{80,32},{96,48},{112,0},{1... | collective-permute-start | bytes 589832 | tf_op jit(solution)/shard_map/ppermute | solution.py:622
  35.9 22.2 %collective-permute-start.5 = (bf16[128,768]{1,0:T(8,128)(2,1)S(1)}, bf16[128,768]{1,0:T(8,128)(2,1)S(1)}, u32[]{:S(2)}, u32[]{:S(2)}) collective-permute-start(bf16[128,768]{1,0:T(8,128)(2,1)S(1)} %fusion.3.refs_0_), channel_id=1, source_target_pairs={{0,96},{16,112},{32,64},{48,80},{64,32},{80,48},{96,0},{112,16},{1... | collective-permute-start | bytes 589832 | tf_op jit(solution)/shard_map/ppermute | solution.py:622
  37.5 24.7 %collective-permute-start.6 = (bf16[128,768]{1,0:T(8,128)(2,1)S(1)}, bf16[128,768]{1,0:T(8,128)(2,1)S(1)}, u32[]{:S(2)}, u32[]{:S(2)}) collective-permute-start(bf16[128,768]{1,0:T(8,128)(2,1)S(1)} %fusion.3.refs_0_), channel_id=1, source_target_pairs={{0,112},{16,64},{32,80},{48,96},{64,48},{80,0},{96,16},{112,32},{1... | collective-permute-start | bytes 589832 | tf_op jit(solution)/shard_map/ppermute | solution.py:622
  75.1 13.2 %collective-permute-start.9 = (bf16[128,768]{1,0:T(8,128)(2,1)S(1)}, bf16[128,768]{1,0:T(8,128)(2,1)S(1)}, u32[]{:S(2)}, u32[]{:S(2)}) collective-permute-start(bf16[128,768]{1,0:T(8,128)(2,1)S(1)} %get-tuple-element.110), channel_id=1, source_target_pairs={{0,16},{16,32},{32,48},{48,0},{64,80},{80,96},{96,112},{112,64},{1... | collective-permute-start | bytes 589832 | tf_op jit(solution)/shard_map/ppermute | solution.py:643
  75.3 12.9 %collective-permute-start.8 = (bf16[128,768]{1,0:T(8,128)(2,1)S(1)}, bf16[128,768]{1,0:T(8,128)(2,1)S(1)}, u32[]{:S(2)}, u32[]{:S(2)}) collective-permute-start(bf16[128,768]{1,0:T(8,128)(2,1)S(1)} %get-tuple-element.111), channel_id=1, source_target_pairs={{0,32},{16,48},{32,0},{48,16},{64,96},{80,112},{96,64},{112,80},{1... | collective-permute-start | bytes 589832 | tf_op jit(solution)/shard_map/ppermute | solution.py:643
  77.3 11.6 %collective-permute-start.7 = (bf16[128,768]{1,0:T(8,128)(2,1)S(1)}, bf16[128,768]{1,0:T(8,128)(2,1)S(1)}, u32[]{:S(2)}, u32[]{:S(2)}) collective-permute-start(bf16[128,768]{1,0:T(8,128)(2,1)S(1)} %get-tuple-element.109), channel_id=1, source_target_pairs={{0,48},{16,0},{32,16},{48,32},{64,112},{80,64},{96,80},{112,96},{1... | collective-permute-start | bytes 589832 | tf_op jit(solution)/shard_map/ppermute | solution.py:643
  107.9 30.0 %collective-permute-start.10 = (bf16[256,1536]{1,0:T(8,128)(2,1)}, bf16[256,1536]{1,0:T(8,128)(2,1)S(1)}, u32[]{:S(2)}, u32[]{:S(2)}) collective-permute-start(bf16[256,1536]{1,0:T(8,128)(2,1)} %bitcast.19.rows_ref.rows_a), channel_id=1, source_target_pairs={{0,16},{16,32},{32,48},{48,0},{64,80},{80,96},{96,112},{112,64},{1... | collective-permute-start | bytes 2359304 | tf_op jit(solution)/shard_map/ppermute | solution.py:669
  109.6 28.3 %collective-permute-start.11 = (bf16[256,1536]{1,0:T(8,128)(2,1)}, bf16[256,1536]{1,0:T(8,128)(2,1)S(1)}, u32[]{:S(2)}, u32[]{:S(2)}) collective-permute-start(bf16[256,1536]{1,0:T(8,128)(2,1)} %bitcast.19.rows_ref.rows_a), channel_id=1, source_target_pairs={{0,48},{16,0},{32,16},{48,32},{64,112},{80,64},{96,80},{112,96},{1... | collective-permute-start | bytes 2359304 | tf_op jit(solution)/shard_map/ppermute | solution.py:669
  120.6 17.3 %all-to-all-start.3 = ((bf16[16,16,1536]{2,1,0:T(8,128)(2,1)}), bf16[16,16,1536]{2,1,0:T(8,128)(2,1)S(1)}, u32[]{:S(2)}, u32[]{:S(2)}) async-start(bf16[16,16,1536]{2,1,0:T(8,128)(2,1)} %bitcast.85), calls=%async_computation.3 | async-start | bytes 1572864 | tf_op jit(solution)/shard_map/all_to_all | solution.py:582
  124.4 23.0 %collective-permute-start.12 = (bf16[256,1536]{1,0:T(8,128)(2,1)}, bf16[256,1536]{1,0:T(8,128)(2,1)}, u32[]{:S(2)}, u32[]{:S(2)}) collective-permute-start(bf16[256,1536]{1,0:T(8,128)(2,1)} %bitcast.19.rows_ref.rows_a), channel_id=1, source_target_pairs={{0,32},{16,48},{32,0},{48,16},{64,96},{80,112},{96,64},{112,80},{1... | collective-permute-start | bytes 2359304 | tf_op jit(solution)/shard_map/ppermute | solution.py:669
  141.5 16.7 %collective-permute-start.13 = (bf16[144,768]{1,0:T(8,128)(2,1)S(1)}, bf16[144,768]{1,0:T(8,128)(2,1)S(1)}, u32[]{:S(2)}, u32[]{:S(2)}) collective-permute-start(bf16[144,768]{1,0:T(8,128)(2,1)S(1)} %get-tuple-element.119), channel_id=1, source_target_pairs={{0,16},{16,32},{32,48},{48,0},{64,80},{80,96},{96,112},{112,64},{1... | collective-permute-start | bytes 663560 | tf_op jit(solution)/shard_map/ppermute | solution.py:711
  142.0 16.2 %collective-permute-start.14 = (bf16[144,768]{1,0:T(8,128)(2,1)S(1)}, bf16[144,768]{1,0:T(8,128)(2,1)S(1)}, u32[]{:S(2)}, u32[]{:S(2)}) collective-permute-start(bf16[144,768]{1,0:T(8,128)(2,1)S(1)} %get-tuple-element.120), channel_id=1, source_target_pairs={{0,32},{16,48},{32,0},{48,16},{64,96},{80,112},{96,64},{112,80},{1... | collective-permute-start | bytes 663560 | tf_op jit(solution)/shard_map/ppermute | solution.py:711
  144.4 13.8 %collective-permute-start.15 = (bf16[144,768]{1,0:T(8,128)(2,1)S(1)}, bf16[144,768]{1,0:T(8,128)(2,1)S(1)}, u32[]{:S(2)}, u32[]{:S(2)}) collective-permute-start(bf16[144,768]{1,0:T(8,128)(2,1)S(1)} %get-tuple-element.118), channel_id=1, source_target_pairs={{0,48},{16,0},{32,16},{48,32},{64,112},{80,64},{96,80},{112,96},{1... | collective-permute-start | bytes 663560 | tf_op jit(solution)/shard_map/ppermute | solution.py:711
  158.3 31.5 %all-to-all-start.4 = ((bf16[8,96,768]{2,1,0:T(8,128)(2,1)}), bf16[8,96,768]{2,1,0:T(8,128)(2,1)S(1)}, u32[]{:S(2)}, u32[]{:S(2)}) async-start(bf16[8,96,768]{2,1,0:T(8,128)(2,1)} %get-tuple-element.84), calls=%async_computation.4 | async-start | bytes 2359296 | tf_op jit(solution)/shard_map/all_to_all | solution.py:582
  175.2 14.5 %collective-permute-start.16 = (bf16[512,384]{1,0:T(8,128)(2,1)}, bf16[512,384]{1,0:T(8,128)(2,1)}, u32[]{:S(2)}, u32[]{:S(2)}) collective-permute-start(bf16[512,384]{1,0:T(8,128)(2,1)} %get-tuple-element.83), channel_id=1, source_target_pairs={{0,64},{16,80},{32,96},{48,112},{64,0},{80,16},{96,32},{112,48},{1... | collective-permute-start | bytes 1179656 | tf_op jit(solution)/shard_map/ppermute | solution.py:721
  190.8 27.0 %all-to-all-start.5 = ((bf16[16,136,384]{2,1,0:T(8,128)(2,1)}), bf16[16,136,384]{2,1,0:T(8,128)(2,1)S(1)}, u32[]{:S(2)}, u32[]{:S(2)}) async-start(bf16[16,136,384]{2,1,0:T(8,128)(2,1)} %weight_pieces.1), calls=%async_computation.5 | async-start | bytes 3342336 | tf_op jit(solution)/shard_map/all_to_all | solution.py:582
  198.6 26.9 %collective-permute-start.17 = (bf16[128,768]{1,0:T(8,128)(2,1)}, bf16[128,768]{1,0:T(8,128)(2,1)}, u32[]{:S(2)}, u32[]{:S(2)}) collective-permute-start(bf16[128,768]{1,0:T(8,128)(2,1)} %get-tuple-element.87), channel_id=1, source_target_pairs={{0,48},{16,0},{32,16},{48,32},{64,112},{80,64},{96,80},{112,96},{1... | collective-permute-start | bytes 589832 | tf_op jit(solution)/shard_map/ppermute | solution.py:730
  199.9 25.6 %collective-permute-start.18 = (bf16[128,768]{1,0:T(8,128)(2,1)}, bf16[128,768]{1,0:T(8,128)(2,1)}, u32[]{:S(2)}, u32[]{:S(2)}) collective-permute-start(bf16[128,768]{1,0:T(8,128)(2,1)} %get-tuple-element.88), channel_id=1, source_target_pairs={{0,32},{16,48},{32,0},{48,16},{64,96},{80,112},{96,64},{112,80},{1... | collective-permute-start | bytes 589832 | tf_op jit(solution)/shard_map/ppermute | solution.py:730
  201.3 24.2 %collective-permute-start.19 = (bf16[128,768]{1,0:T(8,128)(2,1)}, bf16[128,768]{1,0:T(8,128)(2,1)}, u32[]{:S(2)}, u32[]{:S(2)}) collective-permute-start(bf16[128,768]{1,0:T(8,128)(2,1)} %get-tuple-element.89), channel_id=1, source_target_pairs={{0,16},{16,32},{32,48},{48,0},{64,80},{80,96},{96,112},{112,64},{1... | collective-permute-start | bytes 589832 | tf_op jit(solution)/shard_map/ppermute | solution.py:730
  221.4 14.1 %all-to-all-start.6 = ((bf16[8,64,384]{2,1,0:T(8,128)(2,1)}), bf16[8,64,384]{2,1,0:T(8,128)(2,1)S(1)}, u32[]{:S(2)}, u32[]{:S(2)}) async-start(bf16[8,64,384]{2,1,0:T(8,128)(2,1)} %regroup.1), calls=%async_computation.6 | async-start | bytes 786432 | tf_op jit(solution)/shard_map/all_to_all | solution.py:582
  225.6 20.6 %collective-permute-start.20 = (bf16[384,768]{1,0:T(8,128)(2,1)}, bf16[384,768]{1,0:T(8,128)(2,1)}, u32[]{:S(2)}, u32[]{:S(2)}) collective-permute-start(bf16[384,768]{1,0:T(8,128)(2,1)} %get-tuple-element.102), channel_id=1, source_target_pairs={{0,64},{16,80},{32,96},{48,112},{64,0},{80,16},{96,32},{112,48},{1... | collective-permute-start | bytes 1769480 | tf_op jit(solution)/shard_map/ppermute | solution.py:737
  (32 other events, 338.4 us)
where the time goes:
time: 249 us; the launch traced here: 248 us
  waiting for transfers between devices  77.2 us (31%)
  starting transfers between devices  72.6 us (29%)
  Pallas kernels  56.9 us (23%)
  blocking collectives  17.6 us (7%)
  other arithmetic  10.7 us (4%)
  local copies, waits for them, and re-layouts  8.33 us (3%)
  matrix products  3.88 us (2%)
    all_to_all x6, starting transfers between devices, swap(): return lax.all_to_all(chunks, axis, split_axis=0, concat_axis=0, tiled=True)  30.4 us
    all_to_all x6, waiting for transfers between devices, swap(): return lax.all_to_all(chunks, axis, split_axis=0, concat_axis=0, tiled=True)  28.9 us
    ppermute x7, waiting for transfers between devices, body(): lax.ppermute(normed_low, 'ctx', gather_perm(dz, dx))  22.9 us
    ppermute x7, starting transfers between devices, body(): lax.ppermute(normed_low, 'ctx', gather_perm(dz, dx))  19.6 us
    all_to_all x1, blocking collectives, swap(): return lax.all_to_all(chunks, axis, split_axis=0, concat_axis=0, tiled=True)  17.6 us
    pallas_call x1, Pallas kernels, expert_grads(): pl.pallas_call(expert_grads_kernel, grid_spec=pltpu.PrefetchScalarGridSpe...  10.8 us
    pallas_call x1, Pallas kernels, attend_back(): pl.pallas_call(attend_back_kernel, out_shape=[jax.ShapeDtypeStruct(shape,...  10.8 us
    pallas_call x1, Pallas kernels, attend(): pl.pallas_call(attend_kernel, out_shape=[jax.ShapeDtypeStruct(shape, kind...  10.1 us
  transfers between devices with their start and end apart: 27, of which 14 were waited for; matrix products, arithmetic and copies ran while one was open for 4% of the time, Pallas kernels for 19%

commit v1 on v0

--- a/solution.py
+++ b/solution.py
@@ -723,7 +723,10 @@
         me_array, dq, dk, dv, table_local, qkv_weights, attended, pieces, attn_grads
     )
     chunks, taken, columns_last = lax.optimization_barrier((chunks, taken, columns_last))
-    payload = regroup(me_array, swap(chunks, "exp"))
+    collected = swap(chunks, "exp")
+    out_other_grad, _ = lax.optimization_barrier((out_other_grad, collected[0, :1, :1]))
+    out_taken = lax.ppermute(out_other_grad, "ctx", gather_perm(1, 0))
+    payload = regroup(me_array, collected)
 
     normed_grad, *row_low = rows_grad(query_grad, kept, taken, qkv_weights)
     row_parts = [
@@ -733,10 +736,7 @@
     *row_parts, _ = lax.optimization_barrier((*row_parts, payload[0, :1, :1]))
     for part in row_parts:
         normed_grad = normed_grad + part.astype(f32)
-    out_other_grad, _ = lax.optimization_barrier((out_other_grad, payload[0, :1, :1]))
-    out_taken = lax.ppermute(out_other_grad, "ctx", gather_perm(1, 0))
     expert_in_grad = place(columns_last)
-    expert_out_grad = (out_own_grad + out_taken.astype(f32))[None]
     gained_one = normed_grad * attn_norm
     input_grad = (
         mid_grad
@@ -744,8 +744,11 @@
         * (gained_one - scaled_one * jnp.mean(gained_one * scaled_one, axis=-1, keepdims=True))
     )[None]
 
+    last = swap(payload, "ctx")
+    last, out_taken = lax.optimization_barrier((last, out_taken))
+    expert_out_grad = (out_own_grad + out_taken.astype(f32))[None]
     attn_weight_grad, table_row, norm_row, moe_row, router_rows = finish(
-        me_array, swap(payload, "ctx"), attn_norm.reshape(-1, 128)
+        me_array, last, attn_norm.reshape(-1, 128)
     )
     bias_table_grad = table_row.T
     attn_norm_grad = norm_row.reshape(-1)

time: 249 us -> 241 us (0.968)
  waiting for transfers between devices: 77.2 us -> 71.3 us
    ppermute x3, waiting for transfers between devices: 0.01 us -> 7.05 us  [body(): lax.ppermute(low_part, 'ctx', scatter_perm(0, index + 1))]
    ppermute x1, waiting for transfers between devices: 8.17 us -> 1.6 us  [body(): out_taken = lax.ppermute(out_other_grad, 'ctx', gather_perm(1, 0))]
    all_to_all x6, waiting for transfers between devices: 28.9 us -> 22.6 us  [swap(): return lax.all_to_all(chunks, axis, split_axis=0, concat_axis=0, tiled=True)]
    unnamed x60 -> x64, local copies, waits for them, and re-layouts: 5.24 us -> 5.91 us
  transfers between devices with their start and end apart: 27 -> 27, of which waited for: 14 -> 17; matrix products, arithmetic and copies ran while one was open for 4% -> 4% of each run, Pallas kernels for 19% -> 19%
where the time goes in v1:
time: 241 us; the launch traced here: 240 us
  waiting for transfers between devices  71.3 us (30%)
  starting transfers between devices  70.8 us (29%)
  Pallas kernels  56.9 us (24%)
  blocking collectives  17.6 us (7%)
  other arithmetic  9.39 us (4%)
  local copies, waits for them, and re-layouts  9 us (4%)
  matrix products  3.89 us (2%)
    all_to_all x6, starting transfers between devices, swap(): return lax.all_to_all(chunks, axis, split_axis=0, concat_axis=0, tiled=True)  30.4 us
    ppermute x7, waiting for transfers between devices, body(): lax.ppermute(normed_low, 'ctx', gather_perm(dz, dx))  22.9 us
    all_to_all x6, waiting for transfers between devices, swap(): return lax.all_to_all(chunks, axis, split_axis=0, concat_axis=0, tiled=True)  22.6 us
    ppermute x7, starting transfers between devices, body(): lax.ppermute(normed_low, 'ctx', gather_perm(dz, dx))  19.6 us
    all_to_all x1, blocking collectives, swap(): return lax.all_to_all(chunks, axis, split_axis=0, concat_axis=0, tiled=True)  17.6 us
    pallas_call x1, Pallas kernels, attend_back(): pl.pallas_call(attend_back_kernel, out_shape=[jax.ShapeDtypeStruct(shape,...  10.8 us
    pallas_call x1, Pallas kernels, expert_grads(): pl.pallas_call(expert_grads_kernel, grid_spec=pltpu.PrefetchScalarGridSpe...  10.8 us
    pallas_call x1, Pallas kernels, attend(): pl.pallas_call(attend_kernel, out_shape=[jax.ShapeDtypeStruct(shape, kind...  10 us
  transfers between devices with their start and end apart: 27, of which 17 were waited for; matrix products, arithmetic and copies ran while one was open for 4% of the time, Pallas kernels for 19%

profile of v1, /device:TPU:0, one launch (start us, length us, event | category | flops | bytes accessed | tf_op | source)
XLA Modules:
  0.0 240.1 jit_solution(17548359306601342997)
XLA Ops:
  2.2 7.7 %all-to-all-start = ((bf16[8,24,768]{2,1,0:T(8,128)(2,1)}), bf16[8,24,768]{2,1,0:T(8,128)(2,1)S(1)}, u32[]{:S(2)}, u32[]{:S(2)}) async-start(bf16[8,24,768]{2,1,0:T(8,128)(2,1)} %broadcast_in_dim.32), calls=%async_computation | async-start | bytes 589824 | tf_op jit(solution)/shard_map/all_to_all | solution.py:582
  26.7 5.0 %all-to-all-start.1 = ((bf16[16,5,24,384]{3,2,1,0:T(8,128)(2,1)}), bf16[16,5,24,384]{3,2,1,0:T(8,128)(2,1)S(1)}, u32[]{:S(2)}, u32[]{:S(2)}) async-start(bf16[16,5,24,384]{3,2,1,0:T(8,128)(2,1)} %broadcast_in_dim.33), calls=%async_computation.1 | async-start | bytes 2949120 | tf_op jit(solution)/shard_map/all_to_all | solution.py:582
  31.7 4.1 %collective-permute-start.4 = (bf16[128,768]{1,0:T(8,128)(2,1)S(1)}, bf16[128,768]{1,0:T(8,128)(2,1)S(1)}, u32[]{:S(2)}, u32[]{:S(2)}) collective-permute-start(bf16[128,768]{1,0:T(8,128)(2,1)S(1)} %fusion.3.refs_0_), channel_id=1, source_target_pairs={{0,80},{16,96},{32,112},{48,64},{64,16},{80,32},{96,48},{112,0},{1... | collective-permute-start | bytes 589832 | tf_op jit(solution)/shard_map/ppermute | solution.py:622
  37.5 4.7 %collective-permute-start.6 = (bf16[128,768]{1,0:T(8,128)(2,1)S(1)}, bf16[128,768]{1,0:T(8,128)(2,1)S(1)}, u32[]{:S(2)}, u32[]{:S(2)}) collective-permute-start(bf16[128,768]{1,0:T(8,128)(2,1)S(1)} %fusion.3.refs_0_), channel_id=1, source_target_pairs={{0,112},{16,64},{32,80},{48,96},{64,48},{80,0},{96,16},{112,32},{1... | collective-permute-start | bytes 589832 | tf_op jit(solution)/shard_map/ppermute | solution.py:622
  43.1 5.8 %collective-permute-done.4.refs_5_ = bf16[128,768]{1,0:T(8,128)(2,1)S(1)} collective-permute-done((bf16[128,768]{1,0:T(8,128)(2,1)S(1)}, bf16[128,768]{1,0:T(8,128)(2,1)S(1)}, u32[]{:S(2)}, u32[]{:S(2)}) %collective-permute-start.4) | collective-permute-done | bytes 196640 | tf_op jit(solution)/shard_map/ppermute | solution.py:622
  48.9 9.3 %collective-permute-done.5.refs_6_ = bf16[128,768]{1,0:T(8,128)(2,1)S(1)} collective-permute-done((bf16[128,768]{1,0:T(8,128)(2,1)S(1)}, bf16[128,768]{1,0:T(8,128)(2,1)S(1)}, u32[]{:S(2)}, u32[]{:S(2)}) %collective-permute-start.5) | collective-permute-done | bytes 196640 | tf_op jit(solution)/shard_map/ppermute | solution.py:622
  58.1 4.1 %collective-permute-done.6.refs_7_ = bf16[128,768]{1,0:T(8,128)(2,1)S(1)} collective-permute-done((bf16[128,768]{1,0:T(8,128)(2,1)S(1)}, bf16[128,768]{1,0:T(8,128)(2,1)S(1)}, u32[]{:S(2)}, u32[]{:S(2)}) %collective-permute-start.6) | collective-permute-done | bytes 196640 | tf_op jit(solution)/shard_map/ppermute | solution.py:622
  63.4 10.0 %attend.1 = (bf16[192,512]{1,0:T(8,128)(2,1)}, bf16[512,192]{1,0:T(8,128)(2,1)}, bf16[1024,192]{1,0:T(8,128)(2,1)}, bf16[1024,192]{1,0:T(8,128)(2,1)}, f32[3,1,5...) custom-call(s32[1]{0:T(128)} %bitcast.1.me_ref, ...), custom_call_target="tpu_custom_call" | custom-call | tf_op jit(solution)/shard_map/attend/pallas_call | solution.py:458
  79.6 8.6 %collective-permute-done.9 = bf16[128,768]{1,0:T(8,128)(2,1)S(1)} collective-permute-done((bf16[128,768]{1,0:T(8,128)(2,1)S(1)}, bf16[128,768]{1,0:T(8,128)(2,1)S(1)}, u32[]{:S(2)}, u32[]{:S(2)}) %collective-permute-start.9) | collective-permute-done | bytes 196640 | tf_op jit(solution)/shard_map/ppermute | solution.py:643
  90.3 17.6 %all_to_all.35 = bf16[16,16,1536]{2,1,0:T(8,128)(2,1)} all-to-all(bf16[16,16,1536]{2,1,0:T(8,128)(2,1)S(1)} %bitcast.83), channel_id=1, replica_groups=mesh['ctx'=8,'exp'=16] {'exp'}, dimensions={0} | all-to-all | bytes 1572864 | tf_op jit(solution)/shard_map/all_to_all | solution.py:582
  111.1 9.5 %expert.1 = bf16[256,1536]{1,0:T(8,128)(2,1)} custom-call(bf16[256,1536]{1,0:T(8,128)(2,1)} %bitcast.19.rows_ref.rows_a, bf16[768,3072]{1,0:T(8,128)(2,1)} %bitcast.78, bf16[3072,768]{1,0:T(8,128)(2,1)} %bitcast.80), custom_call_target="tpu_custom_call" | custom-call | tf_op jit(solution)/shard_map/expert/pallas_call | solution.py:362
  120.6 3.6 %all-to-all-start.3 = ((bf16[16,16,1536]{2,1,0:T(8,128)(2,1)}), bf16[16,16,1536]{2,1,0:T(8,128)(2,1)S(1)}, u32[]{:S(2)}, u32[]{:S(2)}) async-start(bf16[16,16,1536]{2,1,0:T(8,128)(2,1)} %bitcast.84), calls=%async_computation.3 | async-start | bytes 1572864 | tf_op jit(solution)/shard_map/all_to_all | solution.py:582
  125.5 12.3 %all-to-all-done.3 = bf16[16,16,1536]{2,1,0:T(8,128)(2,1)S(1)} async-done(((bf16[16,16,1536]{2,1,0:T(8,128)(2,1)}), bf16[16,16,1536]{2,1,0:T(8,128)(2,1)S(1)}, u32[]{:S(2)}, u32[]{:S(2)}) %all-to-all-start.3) | async-done | bytes 786464 | tf_op jit(solution)/shard_map/all_to_all | solution.py:582
  147.4 10.8 %expert_grads.1 = (bf16[8,96,768]{2,1,0:T(8,128)(2,1)}, f32[384,768]{1,0:T(8,128)}, bf16[384,768]{1,0:T(8,128)(2,1)}) custom-call(s32[1]{0:T(128)} %bitcast.1.me_ref, bf16[256,1536]{1,0:T(8,128)(2,1)} %bitcast.19.rows_ref.rows_a, bf16[256,1536]{1,0:T(8,128)(2,1)} %copy-done.23, bf16[256,1536]{1,0:T(8,128)(2,1)} %collective-permute-done.12.rows_c, ...), custom_call_target="tpu_custom_call" | custom-call | tf_op jit(solution)/shard_map/expert_grads/pallas_call | solution.py:411
  158.2 6.1 %all-to-all-start.4 = ((bf16[8,96,768]{2,1,0:T(8,128)(2,1)}), bf16[8,96,768]{2,1,0:T(8,128)(2,1)S(1)}, u32[]{:S(2)}, u32[]{:S(2)}) async-start(bf16[8,96,768]{2,1,0:T(8,128)(2,1)} %get-tuple-element.85), calls=%async_computation.4 | async-start | bytes 2359296 | tf_op jit(solution)/shard_map/all_to_all | solution.py:582
  164.4 10.8 %attend_back.1 = (bf16[192,512]{1,0:T(8,128)(2,1)}, bf16[1024,192]{1,0:T(8,128)(2,1)}, bf16[1024,192]{1,0:T(8,128)(2,1)}, bf16[512,192]{1,0:T(8,128)(2,1)}, bf16...) custom-call(s32[1]{0:T(128)} %bitcast.1.me_ref, s32[16]{0:T(128)} %bitcast.93, ...), custom_call_target="tpu_custom_call" | custom-call | tf_op jit(solution)/shard_map/attend_back/pallas_call | solution.py:481
  175.2 3.5 %collective-permute-start.16 = (bf16[512,384]{1,0:T(8,128)(2,1)}, bf16[512,384]{1,0:T(8,128)(2,1)}, u32[]{:S(2)}, u32[]{:S(2)}) collective-permute-start(bf16[512,384]{1,0:T(8,128)(2,1)} %get-tuple-element.84), channel_id=1, source_target_pairs={{0,64},{16,80},{32,96},{48,112},{64,0},{80,16},{96,32},{112,48},{1... | collective-permute-start | bytes 1179656 | tf_op jit(solution)/shard_map/ppermute | solution.py:721
  178.7 5.2 %weight_pieces.1 = bf16[16,136,384]{2,1,0:T(8,128)(2,1)} custom-call(s32[1]{0:T(128)} %bitcast.1.me_ref, bf16[192,512]{1,0:T(8,128)(2,1)} %get-tuple-element.79.dq_ref, bf16[1024,192]{1,0:T(8,128)(2,1)} %get-tuple-element.80.dk_ref, bf16[1024,192]{1,0:T(8,128)(2,1)} %get-tuple-element.81.dv_ref, f32[3,32,128]{2,1,0:T(8,128)} %get-tuple-element.82.table_ref, ...), custom_call_target="tpu_custom_call" | custom-call | tf_op jit(solution)/shard_map/weight_pieces/pallas_call | solution.py:498
  183.9 5.8 %collective-permute-done.16.taken_ref = bf16[512,384]{1,0:T(8,128)(2,1)} collective-permute-done((bf16[512,384]{1,0:T(8,128)(2,1)}, bf16[512,384]{1,0:T(8,128)(2,1)}, u32[]{:S(2)}, u32[]{:S(2)}) %collective-permute-start.16) | collective-permute-done | bytes 393248 | tf_op jit(solution)/shard_map/ppermute | solution.py:721
  190.7 3.9 %all-to-all-start.5 = ((bf16[16,136,384]{2,1,0:T(8,128)(2,1)}), bf16[16,136,384]{2,1,0:T(8,128)(2,1)S(1)}, u32[]{:S(2)}, u32[]{:S(2)}) async-start(bf16[16,136,384]{2,1,0:T(8,128)(2,1)} %weight_pieces.1), calls=%async_computation.5 | async-start | bytes 3342336 | tf_op jit(solution)/shard_map/all_to_all | solution.py:582
  194.6 4.0 %rows_grad.1 = (f32[128,768]{1,0:T(8,128)}, bf16[128,768]{1,0:T(8,128)(2,1)}, bf16[128,768]{1,0:T(8,128)(2,1)}, bf16[128,768]{1,0:T(8,128)(2,1)}) custom-call(bf16[512,192]{1,0:T(8,128)(2,1)} %get-tuple-element.77.query_ref, bf16[512,384]{1,0:T(8,128)(2,1)} %get-tuple-element.78.keep_ref, bf16[512,384]{1,0:T(8,128)(2,1)} %collective-permute-done.16.taken_ref, ...), custom_call_target="tpu_custom_call" | custom-call | tf_op jit(solution)/shard_map/rows_grad/pallas_call | solution.py:294
  213.7 4.0 %all-to-all-done.5.chunk_ref = bf16[16,136,384]{2,1,0:T(8,128)(2,1)S(1)} async-done(((bf16[16,136,384]{2,1,0:T(8,128)(2,1)}), bf16[16,136,384]{2,1,0:T(8,128)(2,1)S(1)}, u32[]{:S(2)}, u32[]{:S(2)}) %all-to-all-start.5) | async-done | bytes 1671200 | tf_op jit(solution)/shard_map/all_to_all | solution.py:582
  221.4 4.0 %all-to-all-start.6 = ((bf16[8,64,384]{2,1,0:T(8,128)(2,1)}), bf16[8,64,384]{2,1,0:T(8,128)(2,1)S(1)}, u32[]{:S(2)}, u32[]{:S(2)}) async-start(bf16[8,64,384]{2,1,0:T(8,128)(2,1)} %regroup.1), calls=%async_computation.6 | async-start | bytes 786432 | tf_op jit(solution)/shard_map/all_to_all | solution.py:582
  229.2 6.2 %all-to-all-done.6.last_ref = bf16[8,64,384]{2,1,0:T(8,128)(2,1)S(1)} async-done(((bf16[8,64,384]{2,1,0:T(8,128)(2,1)}), bf16[8,64,384]{2,1,0:T(8,128)(2,1)S(1)}, u32[]{:S(2)}, u32[]{:S(2)}) %all-to-all-start.6) | async-done | bytes 393248 | tf_op jit(solution)/shard_map/all_to_all | solution.py:582
  (143 shorter events, 72.2 us)
Async XLA Ops:
  2.2 19.0 %all-to-all-start = ((bf16[8,24,768]{2,1,0:T(8,128)(2,1)}), bf16[8,24,768]{2,1,0:T(8,128)(2,1)S(1)}, u32[]{:S(2)}, u32[]{:S(2)}) async-start(bf16[8,24,768]{2,1,0:T(8,128)(2,1)} %broadcast_in_dim.32), calls=%async_computation | async-start | bytes 589824 | tf_op jit(solution)/shard_map/all_to_all | solution.py:582
  12.0 10.0 %collective-permute-start = (bf16[128,768]{1,0:T(8,128)(2,1)S(1)}, bf16[128,768]{1,0:T(8,128)(2,1)S(1)}, u32[]{:S(2)}, u32[]{:S(2)}) collective-permute-start(bf16[128,768]{1,0:T(8,128)(2,1)S(1)} %fusion.3.refs_0_), channel_id=1, source_target_pairs={{0,16},{16,32},{32,48},{48,0},{64,80},{80,96},{96,112},{112,64},{1... | collective-permute-start | bytes 589832 | tf_op jit(solution)/shard_map/ppermute | solution.py:622
  14.1 11.2 %collective-permute-start.1 = (bf16[128,768]{1,0:T(8,128)(2,1)S(1)}, bf16[128,768]{1,0:T(8,128)(2,1)S(1)}, u32[]{:S(2)}, u32[]{:S(2)}) collective-permute-start(bf16[128,768]{1,0:T(8,128)(2,1)S(1)} %fusion.3.refs_0_), channel_id=1, source_target_pairs={{0,32},{16,48},{32,0},{48,16},{64,96},{80,112},{96,64},{112,80},{1... | collective-permute-start | bytes 589832 | tf_op jit(solution)/shard_map/ppermute | solution.py:622
  26.7 35.5 %all-to-all-start.1 = ((bf16[16,5,24,384]{3,2,1,0:T(8,128)(2,1)}), bf16[16,5,24,384]{3,2,1,0:T(8,128)(2,1)S(1)}, u32[]{:S(2)}, u32[]{:S(2)}) async-start(bf16[16,5,24,384]{3,2,1,0:T(8,128)(2,1)} %broadcast_in_dim.33), calls=%async_computation.1 | async-start | bytes 2949120 | tf_op jit(solution)/shard_map/all_to_all | solution.py:582
  31.7 17.1 %collective-permute-start.4 = (bf16[128,768]{1,0:T(8,128)(2,1)S(1)}, bf16[128,768]{1,0:T(8,128)(2,1)S(1)}, u32[]{:S(2)}, u32[]{:S(2)}) collective-permute-start(bf16[128,768]{1,0:T(8,128)(2,1)S(1)} %fusion.3.refs_0_), channel_id=1, source_target_pairs={{0,80},{16,96},{32,112},{48,64},{64,16},{80,32},{96,48},{112,0},{1... | collective-permute-start | bytes 589832 | tf_op jit(solution)/shard_map/ppermute | solution.py:622
  35.9 22.2 %collective-permute-start.5 = (bf16[128,768]{1,0:T(8,128)(2,1)S(1)}, bf16[128,768]{1,0:T(8,128)(2,1)S(1)}, u32[]{:S(2)}, u32[]{:S(2)}) collective-permute-start(bf16[128,768]{1,0:T(8,128)(2,1)S(1)} %fusion.3.refs_0_), channel_id=1, source_target_pairs={{0,96},{16,112},{32,64},{48,80},{64,32},{80,48},{96,0},{112,16},{1... | collective-permute-start | bytes 589832 | tf_op jit(solution)/shard_map/ppermute | solution.py:622
  37.5 24.7 %collective-permute-start.6 = (bf16[128,768]{1,0:T(8,128)(2,1)S(1)}, bf16[128,768]{1,0:T(8,128)(2,1)S(1)}, u32[]{:S(2)}, u32[]{:S(2)}) collective-permute-start(bf16[128,768]{1,0:T(8,128)(2,1)S(1)} %fusion.3.refs_0_), channel_id=1, source_target_pairs={{0,112},{16,64},{32,80},{48,96},{64,48},{80,0},{96,16},{112,32},{1... | collective-permute-start | bytes 589832 | tf_op jit(solution)/shard_map/ppermute | solution.py:622
  75.1 13.2 %collective-permute-start.9 = (bf16[128,768]{1,0:T(8,128)(2,1)S(1)}, bf16[128,768]{1,0:T(8,128)(2,1)S(1)}, u32[]{:S(2)}, u32[]{:S(2)}) collective-permute-start(bf16[128,768]{1,0:T(8,128)(2,1)S(1)} %get-tuple-element.112), channel_id=1, source_target_pairs={{0,16},{16,32},{32,48},{48,0},{64,80},{80,96},{96,112},{112,64},{1... | collective-permute-start | bytes 589832 | tf_op jit(solution)/shard_map/ppermute | solution.py:643
  75.3 12.9 %collective-permute-start.8 = (bf16[128,768]{1,0:T(8,128)(2,1)S(1)}, bf16[128,768]{1,0:T(8,128)(2,1)S(1)}, u32[]{:S(2)}, u32[]{:S(2)}) collective-permute-start(bf16[128,768]{1,0:T(8,128)(2,1)S(1)} %get-tuple-element.113), channel_id=1, source_target_pairs={{0,32},{16,48},{32,0},{48,16},{64,96},{80,112},{96,64},{112,80},{1... | collective-permute-start | bytes 589832 | tf_op jit(solution)/shard_map/ppermute | solution.py:643
  77.2 11.6 %collective-permute-start.7 = (bf16[128,768]{1,0:T(8,128)(2,1)S(1)}, bf16[128,768]{1,0:T(8,128)(2,1)S(1)}, u32[]{:S(2)}, u32[]{:S(2)}) collective-permute-start(bf16[128,768]{1,0:T(8,128)(2,1)S(1)} %get-tuple-element.111), channel_id=1, source_target_pairs={{0,48},{16,0},{32,16},{48,32},{64,112},{80,64},{96,80},{112,96},{1... | collective-permute-start | bytes 589832 | tf_op jit(solution)/shard_map/ppermute | solution.py:643
  107.9 30.0 %collective-permute-start.10 = (bf16[256,1536]{1,0:T(8,128)(2,1)}, bf16[256,1536]{1,0:T(8,128)(2,1)S(1)}, u32[]{:S(2)}, u32[]{:S(2)}) collective-permute-start(bf16[256,1536]{1,0:T(8,128)(2,1)} %bitcast.19.rows_ref.rows_a), channel_id=1, source_target_pairs={{0,16},{16,32},{32,48},{48,0},{64,80},{80,96},{96,112},{112,64},{1... | collective-permute-start | bytes 2359304 | tf_op jit(solution)/shard_map/ppermute | solution.py:669
  109.5 28.3 %collective-permute-start.11 = (bf16[256,1536]{1,0:T(8,128)(2,1)}, bf16[256,1536]{1,0:T(8,128)(2,1)S(1)}, u32[]{:S(2)}, u32[]{:S(2)}) collective-permute-start(bf16[256,1536]{1,0:T(8,128)(2,1)} %bitcast.19.rows_ref.rows_a), channel_id=1, source_target_pairs={{0,48},{16,0},{32,16},{48,32},{64,112},{80,64},{96,80},{112,96},{1... | collective-permute-start | bytes 2359304 | tf_op jit(solution)/shard_map/ppermute | solution.py:669
  120.6 17.3 %all-to-all-start.3 = ((bf16[16,16,1536]{2,1,0:T(8,128)(2,1)}), bf16[16,16,1536]{2,1,0:T(8,128)(2,1)S(1)}, u32[]{:S(2)}, u32[]{:S(2)}) async-start(bf16[16,16,1536]{2,1,0:T(8,128)(2,1)} %bitcast.84), calls=%async_computation.3 | async-start | bytes 1572864 | tf_op jit(solution)/shard_map/all_to_all | solution.py:582
  124.4 23.0 %collective-permute-start.12 = (bf16[256,1536]{1,0:T(8,128)(2,1)}, bf16[256,1536]{1,0:T(8,128)(2,1)}, u32[]{:S(2)}, u32[]{:S(2)}) collective-permute-start(bf16[256,1536]{1,0:T(8,128)(2,1)} %bitcast.19.rows_ref.rows_a), channel_id=1, source_target_pairs={{0,32},{16,48},{32,0},{48,16},{64,96},{80,112},{96,64},{112,80},{1... | collective-permute-start | bytes 2359304 | tf_op jit(solution)/shard_map/ppermute | solution.py:669
  141.5 16.6 %collective-permute-start.13 = (bf16[144,768]{1,0:T(8,128)(2,1)S(1)}, bf16[144,768]{1,0:T(8,128)(2,1)S(1)}, u32[]{:S(2)}, u32[]{:S(2)}) collective-permute-start(bf16[144,768]{1,0:T(8,128)(2,1)S(1)} %get-tuple-element.121), channel_id=1, source_target_pairs={{0,16},{16,32},{32,48},{48,0},{64,80},{80,96},{96,112},{112,64},{1... | collective-permute-start | bytes 663560 | tf_op jit(solution)/shard_map/ppermute | solution.py:711
  142.0 16.2 %collective-permute-start.14 = (bf16[144,768]{1,0:T(8,128)(2,1)S(1)}, bf16[144,768]{1,0:T(8,128)(2,1)S(1)}, u32[]{:S(2)}, u32[]{:S(2)}) collective-permute-start(bf16[144,768]{1,0:T(8,128)(2,1)S(1)} %get-tuple-element.122), channel_id=1, source_target_pairs={{0,32},{16,48},{32,0},{48,16},{64,96},{80,112},{96,64},{112,80},{1... | collective-permute-start | bytes 663560 | tf_op jit(solution)/shard_map/ppermute | solution.py:711
  144.4 13.8 %collective-permute-start.15 = (bf16[144,768]{1,0:T(8,128)(2,1)S(1)}, bf16[144,768]{1,0:T(8,128)(2,1)S(1)}, u32[]{:S(2)}, u32[]{:S(2)}) collective-permute-start(bf16[144,768]{1,0:T(8,128)(2,1)S(1)} %get-tuple-element.120), channel_id=1, source_target_pairs={{0,48},{16,0},{32,16},{48,32},{64,112},{80,64},{96,80},{112,96},{1... | collective-permute-start | bytes 663560 | tf_op jit(solution)/shard_map/ppermute | solution.py:711
  158.2 31.5 %all-to-all-start.4 = ((bf16[8,96,768]{2,1,0:T(8,128)(2,1)}), bf16[8,96,768]{2,1,0:T(8,128)(2,1)S(1)}, u32[]{:S(2)}, u32[]{:S(2)}) async-start(bf16[8,96,768]{2,1,0:T(8,128)(2,1)} %get-tuple-element.85), calls=%async_computation.4 | async-start | bytes 2359296 | tf_op jit(solution)/shard_map/all_to_all | solution.py:582
  175.2 14.5 %collective-permute-start.16 = (bf16[512,384]{1,0:T(8,128)(2,1)}, bf16[512,384]{1,0:T(8,128)(2,1)}, u32[]{:S(2)}, u32[]{:S(2)}) collective-permute-start(bf16[512,384]{1,0:T(8,128)(2,1)} %get-tuple-element.84), channel_id=1, source_target_pairs={{0,64},{16,80},{32,96},{48,112},{64,0},{80,16},{96,32},{112,48},{1... | collective-permute-start | bytes 1179656 | tf_op jit(solution)/shard_map/ppermute | solution.py:721
  190.7 27.0 %all-to-all-start.5 = ((bf16[16,136,384]{2,1,0:T(8,128)(2,1)}), bf16[16,136,384]{2,1,0:T(8,128)(2,1)S(1)}, u32[]{:S(2)}, u32[]{:S(2)}) async-start(bf16[16,136,384]{2,1,0:T(8,128)(2,1)} %weight_pieces.1), calls=%async_computation.5 | async-start | bytes 3342336 | tf_op jit(solution)/shard_map/all_to_all | solution.py:582
  199.9 9.5 %collective-permute-start.18 = (bf16[128,768]{1,0:T(8,128)(2,1)}, bf16[128,768]{1,0:T(8,128)(2,1)S(1)}, u32[]{:S(2)}, u32[]{:S(2)}) collective-permute-start(bf16[128,768]{1,0:T(8,128)(2,1)} %get-tuple-element.89), channel_id=1, source_target_pairs={{0,32},{16,48},{32,0},{48,16},{64,96},{80,112},{96,64},{112,80},{1... | collective-permute-start | bytes 589832 | tf_op jit(solution)/shard_map/ppermute | solution.py:733
  201.4 11.4 %collective-permute-start.19 = (bf16[128,768]{1,0:T(8,128)(2,1)}, bf16[128,768]{1,0:T(8,128)(2,1)S(1)}, u32[]{:S(2)}, u32[]{:S(2)}) collective-permute-start(bf16[128,768]{1,0:T(8,128)(2,1)} %get-tuple-element.90), channel_id=1, source_target_pairs={{0,16},{16,32},{32,48},{48,0},{64,80},{80,96},{96,112},{112,64},{1... | collective-permute-start | bytes 589832 | tf_op jit(solution)/shard_map/ppermute | solution.py:733
  201.4 27.9 %collective-permute-start.20 = (bf16[384,768]{1,0:T(8,128)(2,1)}, bf16[384,768]{1,0:T(8,128)(2,1)}, u32[]{:S(2)}, u32[]{:S(2)}) collective-permute-start(bf16[384,768]{1,0:T(8,128)(2,1)} %get-tuple-element.95), channel_id=1, source_target_pairs={{0,64},{16,80},{32,96},{48,112},{64,0},{80,16},{96,32},{112,48},{1... | collective-permute-start | bytes 1769480 | tf_op jit(solution)/shard_map/ppermute | solution.py:728
  221.4 14.0 %all-to-all-start.6 = ((bf16[8,64,384]{2,1,0:T(8,128)(2,1)}), bf16[8,64,384]{2,1,0:T(8,128)(2,1)S(1)}, u32[]{:S(2)}, u32[]{:S(2)}) async-start(bf16[8,64,384]{2,1,0:T(8,128)(2,1)} %regroup.1), calls=%async_computation.6 | async-start | bytes 786432 | tf_op jit(solution)/shard_map/all_to_all | solution.py:582
  (34 other events, 337.4 us)
